TPU v7x, 32 devices: a whole 2x2x4 slice. The times are simulated.
32 devices in a mesh: groups: 2 (over x), blk: 16 (over z, y, core).
Axes of the slice: x: 2, y: 2, z: 4, core: 2. Of those that a mesh axis runs over, the one named last changes fastest.
Arguments:
- residual: bfloat16 [8, 2048, 3072], P('groups', 'blk'), parts along dimension 0, may hold values from -6 to 6
- attention: bfloat16 [8, 2048, 3072], P('groups', 'blk'), parts along dimension 0, may hold values from -6 to 6
- condition: bfloat16 [8, 3072], P('groups'), parts along dimension 0, may hold values from -4 to 4
- proj_weight: bfloat16 [3072, 3072], P('blk'), may hold values from -0.109375 to 0.109375
- mod_weight: bfloat16 [3072, 9216], P('blk'), may hold values from -0.109375 to 0.109375
- residual_cot: bfloat16 [8, 2048, 3072], P('groups', 'blk'), parts along dimension 0, may hold values from -6 to 6
- normed_cot: bfloat16 [8, 2048, 3072], P('groups', 'blk'), parts along dimension 0, may hold values from -6 to 6
Outputs:
- normed_out: bfloat16 [8, 2048, 3072], P('groups', 'blk'), parts along dimension 0
- residual_grad: bfloat16 [8, 2048, 3072], P('groups', 'blk'), parts along dimension 0
- attention_grad: bfloat16 [8, 2048, 3072], P('groups', 'blk'), parts along dimension 0
- condition_grad: float32 [8, 3072], P('groups', 'blk'), parts along dimension 0
There are 2 independent parts, one for each index of `groups`. A program takes and returns all parts, laid end to end along the dimension named above; an argument that names none is the same for every part. Nothing has to cross between parts.
All inputs are finite; a program needn't handle non-finite values.
Results may differ from a plain program's by a relative error of at most 0.006.
Values may be sent and summed in bfloat16 or wider, within the bound.
A program may use at most 128 MiB of HBM per device.

v0:
```python
import math

import jax
import jax.numpy as jnp
from jax import lax
from jax.sharding import PartitionSpec as P

norm_eps = 1e-06


def silu_slope(argument):
    sigmoid_val = jax.nn.sigmoid(argument)
    return sigmoid_val * (1.0 + argument * (1.0 - sigmoid_val))


def local(residual, attention, condition, proj_weight, mod_weight, residual_cot, normed_cot):
    latents, tokens, features = residual.shape
    row_count = latents * tokens
    panel_rows = proj_weight.shape[0]
    device_pos = lax.axis_index("blk")
    seq_len = tokens * lax.axis_size("blk")
    condition_f32 = condition.astype(jnp.float32)
    own_cond = lax.dynamic_slice_in_dim(condition_f32, device_pos * panel_rows, panel_rows, 1)
    own_act = jax.nn.silu(own_cond).astype(jnp.bfloat16)
    modulation = lax.psum(jnp.dot(own_act, mod_weight, preferred_element_type=jnp.float32), "blk")
    gating = modulation[:, None, 0:features]
    shifts = modulation[:, None, features : 2 * features]
    scales = modulation[:, None, 2 * features : 3 * features]
    flat_attn = attention.reshape(row_count, features)
    projected = jnp.dot(
        flat_attn,
        lax.all_gather(proj_weight, "blk", axis=0, tiled=True),
        preferred_element_type=jnp.float32,
    )
    projected = projected.reshape(latents, tokens, features)
    summed = residual.astype(jnp.float32) + gating * projected
    average = jnp.mean(summed, axis=-1, keepdims=True)
    centered = summed - average
    variance = jnp.mean(centered * centered, axis=-1, keepdims=True)
    inverse = lax.rsqrt(variance + norm_eps)
    normed = centered * inverse
    normed_out = ((1.0 + scales) * normed + shifts).astype(jnp.bfloat16)
    cot_f32 = normed_cot.astype(jnp.float32)
    normed_grad = cot_f32 * (1.0 + scales)
    summed_grad = residual_cot.astype(jnp.float32) + inverse * (
        normed_grad
        - jnp.mean(normed_grad, axis=-1, keepdims=True)
        - normed * jnp.mean(normed_grad * normed, axis=-1, keepdims=True)
    )
    residual_grad = summed_grad.astype(jnp.bfloat16)
    scaled = (summed_grad * gating).astype(jnp.bfloat16).reshape(row_count, features)
    attn_grad = jnp.dot(
        scaled,
        lax.all_gather(proj_weight, "blk", axis=0, tiled=True).T,
        preferred_element_type=jnp.float32,
    )
    attention_grad = attn_grad.astype(jnp.bfloat16).reshape(latents, tokens, features)
    local_grad = jnp.concatenate(
        [
            jnp.sum(summed_grad * projected, axis=1),
            jnp.sum(cot_f32, axis=1),
            jnp.sum(cot_f32 * normed, axis=1),
        ],
        axis=1,
    )
    mod_grad = lax.psum(local_grad, "blk")
    back = jnp.dot(mod_grad, mod_weight.astype(jnp.float32).T, precision=lax.Precision.HIGHEST)
    condition_grad = silu_slope(own_cond) * back / math.sqrt(seq_len)
    return (normed_out, residual_grad, attention_grad, condition_grad)


def solution(mesh):
    in_specs = (
        P("groups", "blk", None),
        P("groups", "blk", None),
        P("groups", None),
        P("blk", None),
        P("blk", None),
        P("groups", "blk", None),
        P("groups", "blk", None),
    )
    out_specs = (
        P("groups", "blk", None),
        P("groups", "blk", None),
        P("groups", "blk", None),
        P("groups", "blk"),
    )
    return jax.shard_map(local, mesh=mesh, in_specs=in_specs, out_specs=out_specs, check_vma=False)
```

profile of v0, /device:TPU:0, one launch (start us, length us, event | category | flops | bytes accessed | tf_op | source)
XLA Modules:
  0.0 331.8 jit_solution(7950972562521541903)
XLA Ops:
  7.2 0.0 copy-start
  7.2 0.0 all-reduce.3.cloned.1.call-start
  7.2 1.9 copy-done
  9.2 2.0 fusion.17
  11.2 0.0 all-reduce.3.cloned.1.call-update
  11.2 0.0 all-gather.2.cloned.1.call-start
  11.2 0.7 all-gather.2.cloned.1.call-update
  11.9 0.0 all-reduce.5.cloned.1.call-start
  12.0 90.5 %all-reduce.3.cloned.1.call-done = f32[4,9216]{1,0:T(4,128)} async-done(((f32[4,9216]{1,0:T(4,128)}), f32[4,9216]{1,0:T(4,128)}) %all-reduce.3.cloned.1.call-update) | async-done | bytes 147472 | tf_op jit(solution)/shard_map/psum | solution.py:25
  102.4 1.5 slice_add_fusion
  103.9 100.0 %all-gather.2.cloned.1.call-done = bf16[3072,3072]{1,0:T(8,128)(2,1)} async-done(((bf16[192,3072]{1,0:T(8,128)(2,1)}), bf16[3072,3072]{1,0:T(8,128)(2,1)}) %all-gather.2.cloned.1.call-update) | async-done | bytes 18874384 | tf_op jit(solution)/shard_map/all_gather | solution.py:32
  203.9 17.1 %fusion.24 = (f32[4,128]{1,0:T(4,128)S(1)}, f32[4,128,3072]{2,1,0:T(8,128)S(1)}, f32[4,128,3072]{2,1,0:T(8,128)}) fusion(f32[4,3072]{1,0:T(4,128)} %get-tuple-element.17, bf16[4,128,3072]{2,1,0:T(8,128)(2,1)} %param.7, bf16[4,128,3072]{2,1,0:T(8,128)(2,1)} %param.8, bf16[3072,3072]{1,0:T(8,128)(2,1)} %all-gather.2.cloned.1.call-done), kind=kOutput, calls=%fused_computation.41 | convolution fusion | flops 9669967872 | bytes 37799936 | tf_op jit(solution)/shard_map/dot_general | solution.py:30
  221.1 0.0 copy-start.1
  221.1 0.0 copy-start.3
  221.1 0.0 slice-start
  221.1 0.8 multiply_reduce_fusion.1
  221.8 0.0 copy-start.2
  221.9 0.0 copy-start.4
  221.9 1.1 copy-done.1
  223.0 0.0 copy-done.3
  223.0 0.0 slice-start.1
  223.0 3.1 fusion.9
  226.1 0.0 slice-done
  226.1 0.0 copy-done.2
  226.1 0.0 copy-done.4
  226.1 0.0 slice-done.1
  226.1 6.2 %multiply_reduce_fusion = (f32[4,3072]{1,0:T(4,128)S(1)}, f32[4,128,3072]{2,1,0:T(8,128)}, bf16[4,128,3072]{2,1,0:T(8,128)(2,1)}) fusion(f32[4,128,3072]{2,1,0:T(8,128)S(1)} %bitcast.14, f32[4,128]{1,0:T(4,128)S(1)} %get-tuple-element.19, f32[4,128,3072]{2,1,0:T(8,128)S(1)} %get-tuple-element.11, f32[4,128]{1,0:T(4,128)S(1)} %broadcast_multiply_fusion.2, ...), kind=kLoop, calls=%fused_computation.13 | loop fusion | flops 23580672 | bytes 28467200 | tf_op jit(solution)/shard_map/reduce_sum | solution.py:60
  232.4 0.7 pad_maximum_fusion
  233.1 0.0 all-reduce.5.cloned.1.call-update
  233.1 7.5 %multiply_convert_fusion = (bf16[4,128,3072]{2,1,0:T(8,128)(2,1)S(1)}, bf16[4,128,3072]{2,1,0:T(8,128)(2,1)}) fusion(f32[4,128,3072]{2,1,0:T(8,128)} %get-tuple-element.9, f32[4,3072]{1,0:T(4,128)} %get-tuple-element.17), kind=kLoop, calls=%fused_computation.14 | loop fusion | flops 4718592 | bytes 12632064 | tf_op jit(solution)/shard_map/convert_element_type | solution.py:51
  240.6 15.0 %convolution_convert_fusion = bf16[512,3072]{1,0:T(8,128)(2,1)} fusion(bf16[512,3072]{1,0:T(8,128)(2,1)S(1)} %bitcast.15, bf16[3072,3072]{1,0:T(8,128)(2,1)} %all-gather.2.cloned.1.call-done), kind=kOutput, calls=%fused_computation.19 | convolution fusion | flops 9665249280 | bytes 25165824 | tf_op jit(solution)/shard_map/dot_general | solution.py:52
  255.6 65.3 %all-reduce.5.cloned.1.call-done = f32[4,9216]{1,0:T(4,128)} async-done(((f32[4,9216]{1,0:T(4,128)}), f32[4,9216]{1,0:T(4,128)}) %all-reduce.5.cloned.1.call-update) | async-done | bytes 147472 | tf_op jit(solution)/shard_map/psum | solution.py:66
  320.9 4.4 %fusion.10 = f32[4,192]{1,0:T(4,128)} fusion(f32[4,9216]{1,0:T(4,128)} %all-reduce.5.cloned.1.call-done, bf16[192,9216]{1,0:T(8,128)(2,1)S(1)} %copy-done, bf16[4,3072]{1,0:T(4,128)(2,1)} %param.9, s32[]{:T(128)S(6)} %select_n.3), kind=kOutput, calls=%fused_computation.21 | convolution fusion | flops 84942336 | bytes 3691012 | tf_op jit(solution)/shard_map/dot_general | solution.py:67
  (4 shorter events, 0.0 us)
Async XLA Ops:
  7.2 2.0 copy-start
  7.2 95.3 %all-reduce.3.cloned.1.call-start = ((), (), s32[]{:S(2)}) async-start(), calls=%async_computation | async-start | bytes 294912 | tf_op jit(solution)/shard_map/psum | solution.py:25
  11.2 192.7 %all-gather.2.cloned.1.call-start = ((), (), s32[]{:S(2)}) async-start(), calls=%async_computation.1 | async-start | bytes 20054016 | tf_op jit(solution)/shard_map/all_gather | solution.py:32
  11.9 309.0 %all-reduce.5.cloned.1.call-start = ((), (), s32[]{:S(2)}) async-start(), calls=%async_computation.2 | async-start | bytes 294912 | tf_op jit(solution)/shard_map/psum | solution.py:66
  221.1 1.9 copy-start.1
  221.1 1.9 copy-start.3
  221.1 5.0 %slice-start = ((s8[6291456]{0:T(1024)(128)(4,1)}), s8[4194304]{0:T(1024)(128)(4,1)S(1)}, s32[]{:S(2)}) async-start(s8[6291456]{0:T(1024)(128)(4,1)} %bitcast.13), calls=%async_computation.3 | async-start | bytes 8388608
  221.8 4.3 %copy-start.2 = (bf16[4,128,3072]{2,1,0:T(8,128)(2,1)S(1)}, bf16[4,128,3072]{2,1,0:T(8,128)(2,1)}, u32[]{:S(2)}) copy-start(bf16[4,128,3072]{2,1,0:T(8,128)(2,1)} %param.12) | copy-start | bytes 9437188
  221.9 4.3 %copy-start.4 = (f32[4,3072]{1,0:T(4,128)S(1)}, f32[4,3072]{1,0:T(4,128)}, u32[]{:S(2)}) copy-start(f32[4,3072]{1,0:T(4,128)} %get-tuple-element.16) | copy-start | bytes 147460
  223.0 3.2 slice-start.1
Sparse Core Ops, SparseCore 0:
  12.0 90.3 all-reduce.2
  104.0 99.8 all-gather.1
  233.2 87.6 all-reduce.4
where the time goes:
time: 332 us
  waiting for transfers between devices  256 us (77%)
  matrix products  38.5 us (12%)
  other arithmetic  19.8 us (6%)
  between operations  13.9 us (4%)
    all_gather x1, waiting for transfers between devices, local(): lax.all_gather(proj_weight, 'blk', axis=0, tiled=True)  100 us
    psum x1, waiting for transfers between devices, local(): lax.psum(jnp.dot(own_act, mod_weight, preferred_element_type=jnp.float32)...  90.5 us
    psum x1, waiting for transfers between devices, local(): mod_grad = lax.psum(local_grad, 'blk')  65.3 us
    dot_general x1, matrix products, local(): jnp.dot(flat_attn, lax.all_gather(proj_weight, 'blk', axis=0, tiled=True)...  17.1 us
    dot_general x1, matrix products, local(): jnp.dot(scaled, lax.all_gather(proj_weight, 'blk', axis=0, tiled=True).T,...  15 us
    convert_element_type x1, other arithmetic, local(): (summed_grad * gating).astype(jnp.bfloat16).reshape(row_count, features)  7.5 us
  transfers between devices with their start and end apart: 3, of which 3 were waited for; matrix products, arithmetic and copies ran while one was open for 7% of the time, Pallas kernels for 0%

commit v1 on v0

v1 whole, which is shorter than its diff:
```python
import functools
import math

import jax
import jax.numpy as jnp
from jax import lax
from jax.experimental import pallas as pl
from jax.experimental.pallas import tpu as pltpu
from jax.sharding import PartitionSpec as P

norm_eps = 1e-06
MESH = pl.DeviceIdType.MESH
F32, BF16 = jnp.float32, jnp.bfloat16
HALVES = 2
COLUMN_BLOCKS = 8
TILE = 32


def kernel(
    groups, blk, latents, tokens,
    res_hbm, att_hbm, cond, w_hbm, modw_hbm, rcot_hbm, ncot_hbm,
    nout_hbm, rgrad_hbm, agrad_hbm, cgrad,
    w, att, res, rcot, ncot, modw, acc, mod, mgrad,
    stage_a, land_a, full_a, stage_b, land_b, full_b,
    load_sem, store_sem, ring_send, ring_recv, sib_send, sib_recv, own_sem,
    rs_send, rs_recv, ag_send, ag_recv,
):
    rows, features = att.shape
    shard = w_hbm.shape[0]
    chip_rows = 2 * shard
    chips = blk // 2
    third = features // 3
    piece = shard // HALVES
    steps = chips - 1
    total = steps * HALVES
    lat_rows = latents * COLUMN_BLOCKS // blk
    mod_cols = 3 * features // COLUMN_BLOCKS
    fold = groups == 2 and chips % 2 == 0

    me = lax.axis_index("blk")
    group = lax.axis_index("groups")
    core = lax.rem(me, 2)
    chip = lax.div(me, 2)
    plane = lax.rem(group, 2)

    if fold:
        side = lax.rem(chip, 2)
        along = lax.div(chip, 2)
        place = jnp.where(side == 0, along, chips - 1 - along)
    else:
        place = chip

    def chip_at(pos):
        pos = lax.rem(pos + 2 * chips, chips)
        if not fold:
            return pos
        return jnp.where(pos < chips // 2, 2 * pos, 2 * (chips - 1 - pos) + 1)

    after = {"blk": 2 * chip_at(place + 1) + core}
    before = {"blk": 2 * chip_at(place - 1) + core}
    sibling = {"blk": me + 1 - 2 * core}
    partner = {"groups": group + 1 - 2 * plane}

    cols = (
        pl.multiple_of((2 - plane) * third, third),
        0,
        pl.multiple_of((1 + plane) * third, third),
    )
    signs = (-1, 1, -1)

    loads = [
        pltpu.make_async_copy(src, dst, load_sem.at[i])
        for i, (src, dst) in enumerate(
            (
                (w_hbm, w.at[pl.ds(pl.multiple_of(me * shard, shard), shard)]),
                (modw_hbm, modw),
                (att_hbm, att),
                (ncot_hbm, ncot),
                (res_hbm, res),
                (rcot_hbm, rcot),
            )
        )
    ]
    for load in loads:
        load.start()

    barrier = pltpu.get_barrier_semaphore()

    def greet(d, carry):
        pl.semaphore_signal(
            barrier, inc=1, device_id={"blk": lax.rem(me + d, blk)}, device_id_type=MESH
        )
        return carry

    lax.fori_loop(1, blk, greet, 0)
    pl.semaphore_signal(barrier, inc=1, device_id=partner, device_id_type=MESH)
    pl.semaphore_wait(barrier, blk)

    def block(step, half, way, of_core):
        owner = chip_at(place + signs[way] * step)
        start = pl.multiple_of((2 * owner + of_core) * shard + half * piece, piece)
        return w.at[pl.ds(start, piece), pl.ds(cols[way], third)]

    def copy(ref, send, recv, device):
        return pltpu.make_async_remote_copy(
            src_ref=ref, dst_ref=ref, send_sem=send, recv_sem=recv,
            device_id=device, device_id_type=MESH,
        )

    def ring(i, way):
        device = (after, before)[way]
        step = lax.div(i, HALVES)
        return copy(
            block(step, lax.rem(i, HALVES), way, core),
            ring_send.at[way, i], ring_recv.at[way, i], device,
        )

    def arrival(i, way):
        step = lax.div(i, HALVES) + 1
        return copy(
            block(step, lax.rem(i, HALVES), way, core),
            ring_send.at[way, i], ring_recv.at[way, i], (after, before)[way],
        )

    def cross_out(i):
        step = lax.div(i, HALVES) + 1
        return copy(
            block(step, lax.rem(i, HALVES), 0, core),
            ring_send.at[2, i], ring_recv.at[2, i], partner,
        )

    def cross_in(i):
        step = lax.div(i, HALVES) + 1
        return copy(
            block(step, lax.rem(i, HALVES), 2, core),
            ring_send.at[2, i], ring_recv.at[2, i], partner,
        )

    def to_sibling(i, way, of_core):
        step = lax.div(i, HALVES) + 1
        return copy(
            block(step, lax.rem(i, HALVES), way, of_core),
            sib_send.at[way, i], sib_recv.at[way, i], sibling,
        )

    def own_to_sibling(of_core):
        start = pl.multiple_of((2 * chip + of_core) * shard, shard)
        return copy(w.at[pl.ds(start, shard)], own_sem.at[0], own_sem.at[1], sibling)

    loads[0].wait()
    for i in range(HALVES):
        ring(i, 0).start()
        ring(i, 1).start()
    own_to_sibling(core).start()

    def scatter(which, stage, land, peer, source):
        return pltpu.make_async_remote_copy(
            src_ref=stage.at[peer], dst_ref=land.at[source],
            send_sem=rs_send.at[which, peer], recv_sem=rs_recv.at[which, source],
            device_id={"blk": peer}, device_id_type=MESH,
        )

    def spread(which, full, peer, source):
        return pltpu.make_async_remote_copy(
            src_ref=full.at[source], dst_ref=full.at[source],
            send_sem=ag_send.at[which, peer], recv_sem=ag_recv.at[which, source],
            device_id={"blk": peer}, device_id_type=MESH,
        )

    def each_peer(do):
        def body(d, carry):
            do(lax.rem(me + d, blk))
            return carry

        lax.fori_loop(1, blk, body, 0)

    def sum_begin(which, values, stage, land):
        for p in range(blk):
            lat = (p // COLUMN_BLOCKS) * lat_rows
            col = (p % COLUMN_BLOCKS) * mod_cols
            stage[p] = values[lat : lat + lat_rows, col : col + mod_cols]
        each_peer(lambda peer: scatter(which, stage, land, peer, me).start())

    def sum_middle(which, stage, land, full):
        each_peer(lambda peer: scatter(which, stage, land, peer, peer).wait_recv())

        def add(d, value):
            return value + land[lax.rem(me + d, blk)]

        full[me] = lax.fori_loop(1, blk, add, stage[me])
        each_peer(lambda peer: spread(which, full, peer, me).start())

    def sum_end(which, stage, land, full, put):
        each_peer(lambda peer: spread(which, full, peer, peer).wait_recv())
        for p in range(blk):
            lat = (p // COLUMN_BLOCKS) * lat_rows
            col = (p % COLUMN_BLOCKS) * mod_cols
            for r in range(lat_rows):
                put(lat + r, col, full[p, r : r + 1, :])
        each_peer(lambda peer: scatter(which, stage, land, peer, me).wait_send())
        each_peer(lambda peer: spread(which, full, peer, me).wait_send())

    loads[1].wait()
    v = cond[...]
    act = (v * jax.nn.sigmoid(v)).astype(BF16)
    sum_begin(0, jnp.dot(act, modw[...], preferred_element_type=F32), stage_a, land_a)

    acc[...] = jnp.zeros_like(acc)
    loads[2].wait()
    overlapped = chip_rows % 128 == 0

    def multiply(step, way):
        if not overlapped:
            return
        owner = chip_at(place + signs[way] * step)
        k = pl.ds(pl.multiple_of(owner * chip_rows, chip_rows), chip_rows)
        wide = third // 2

        @pl.loop(0, 2)
        def _(n):
            c = pl.ds(pl.multiple_of(cols[way] + n * wide, wide), wide)
            acc[:, c] += jnp.dot(att[:, k], w[k, c], preferred_element_type=F32)

    def from_sibling(step, way):
        for h in range(HALVES):
            to_sibling((step - 1) * HALVES + h, way, 1 - core).wait_recv()

    def put_mod(lat, col, values):
        mod[lat, :, pl.ds(col, mod_cols)] = values

    def turn(i, carry):
        step = lax.div(i, HALVES)
        half = lax.rem(i, HALVES)
        for way in range(2):
            arrival(i, way).wait_recv()

            @pl.when(i + HALVES < total)
            def _(way=way):
                ring(i + HALVES, way).start()

            if way == 0:
                cross_out(i).start()
            to_sibling(i, way, core).start()

        @pl.when(i >= 1)
        def _():
            cross_in(i - 1).wait_recv()
            to_sibling(i - 1, 2, core).start()

        @pl.when(i == 0)
        def _():
            own_to_sibling(1 - core).wait_recv()

        @pl.when(half == 0)
        def _():
            @pl.when(step >= 1)
            def _():
                from_sibling(step, 0)
                from_sibling(step, 1)

            multiply(step, 0)
            multiply(step, 1)

        @pl.when(half == HALVES - 1)
        def _():
            @pl.when(step >= 1)
            def _():
                from_sibling(step, 2)

            multiply(step, 2)

        @pl.when(i == 1)
        def _():
            sum_middle(0, stage_a, land_a, full_a)

        @pl.when(i == 5)
        def _():
            sum_end(0, stage_a, land_a, full_a, put_mod)

        return carry

    lax.fori_loop(0, total, turn, 0)
    cross_in(total - 1).wait_recv()
    to_sibling(total - 1, 2, core).start()
    from_sibling(steps, 0)
    multiply(steps, 0)
    from_sibling(steps, 1)
    multiply(steps, 1)
    from_sibling(steps, 2)
    multiply(steps, 2)

    if not overlapped:
        @pl.loop(0, features // 256)
        def _(n):
            c = pl.ds(pl.multiple_of(n * 256, 256), 256)
            acc[:, c] = jnp.dot(att[...], w[:, c], preferred_element_type=F32)

    for load in loads[3:]:
        load.wait()
    mgrad[...] = jnp.zeros_like(mgrad)
    chunks = features // 128

    def norm(t, carry):
        lat = lax.div(t * TILE, tokens)
        r = pl.ds(pl.multiple_of(t * TILE, TILE), TILE)

        def parts(j):
            c = pl.ds(j * 128, 128)
            gate = mod[lat, :, pl.ds(j * 128, 128)]
            scale = 1.0 + mod[lat, :, pl.ds(2 * features + j * 128, 128)]
            proj = acc[r, c]
            summed = res[r, c].astype(F32) + gate * proj
            cot = ncot[r, c].astype(F32)
            return c, gate, scale, proj, summed, cot

        zero = jnp.zeros((TILE, 128), F32)
        one, two = zero, zero
        for j in range(chunks):
            _, _, scale, _, summed, cot = parts(j)
            one += summed
            two += cot * scale
        average = jnp.sum(one, axis=1, keepdims=True) / features
        grad_mean = jnp.sum(two, axis=1, keepdims=True) / features
        one, two = zero, zero
        for j in range(chunks):
            _, _, scale, _, summed, cot = parts(j)
            centered = summed - average
            one += centered * centered
            two += cot * scale * centered
        inverse = lax.rsqrt(jnp.sum(one, axis=1, keepdims=True) / features + norm_eps)
        grad_norm = inverse * (jnp.sum(two, axis=1, keepdims=True) / features)
        for j in range(chunks):
            c, gate, scale, proj, summed, cot = parts(j)
            normed = (summed - average) * inverse
            shift = mod[lat, :, pl.ds(features + j * 128, 128)]
            grad = rcot[r, c].astype(F32) + inverse * (
                cot * scale - grad_mean - normed * grad_norm
            )
            res[r, c] = (scale * normed + shift).astype(BF16)
            rcot[r, c] = grad.astype(BF16)
            att[r, c] = (grad * gate).astype(BF16)

            def fold_rows(value):
                return jnp.sum(value.reshape(TILE // 8, 8, 128), axis=0)

            for b, value in enumerate((grad * proj, cot, cot * normed)):
                mgrad[lat, :, pl.ds(b * features + j * 128, 128)] += fold_rows(value)
        return carry

    lax.fori_loop(0, rows // TILE, norm, 0)

    stores = [
        pltpu.make_async_copy(res, nout_hbm, store_sem.at[0]),
        pltpu.make_async_copy(rcot, rgrad_hbm, store_sem.at[1]),
    ]
    for store in stores:
        store.start()

    sum_begin(1, jnp.sum(mgrad[...], axis=1), stage_b, land_b)

    tiles = 8
    width = features // tiles

    def back_store(n):
        c = pl.ds(pl.multiple_of(n * width, width), width)
        return pltpu.make_async_copy(ncot.at[:, c], agrad_hbm.at[:, c], store_sem.at[2 + n])

    def back(n, carry):
        k = pl.ds(pl.multiple_of(n * width, width), width)
        ncot[:, k] = lax.dot_general(
            att[...], w[k, :], (((1,), (1,)), ((), ())), preferred_element_type=F32
        ).astype(BF16)
        back_store(n).start()

        @pl.when(n == 2)
        def _():
            sum_middle(1, stage_b, land_b, full_b)

        return carry

    lax.fori_loop(0, tiles, back, 0)

    def put_grad(lat, col, values):
        mod[lat, :, pl.ds(col, mod_cols)] = values

    sum_end(1, stage_b, land_b, full_b, put_grad)
    grads = jnp.concatenate([mod[i] for i in range(latents)], axis=0)
    upper = grads.astype(BF16).astype(F32)
    both = jnp.concatenate([upper, grads - upper], axis=0).astype(BF16)
    product = lax.dot_general(
        both, modw[...], (((1,), (1,)), ((), ())), preferred_element_type=F32
    )
    back_sum = product[:latents] + product[latents:]
    gate = jax.nn.sigmoid(v)
    slope = gate * (1.0 + v * (1.0 - gate))
    cgrad[...] = slope * back_sum / math.sqrt(tokens * blk)

    def finish(i, carry):
        ring(i, 0).wait_send()
        ring(i, 1).wait_send()
        cross_out(i).wait_send()
        for way in range(3):
            to_sibling(i, way, core).wait_send()
        return carry

    lax.fori_loop(0, total, finish, 0)
    own_to_sibling(core).wait_send()
    for store in stores:
        store.wait()

    def drain(n, carry):
        back_store(n).wait()
        return carry

    lax.fori_loop(0, tiles, drain, 0)


def local(groups, blk, residual, attention, condition, proj_weight, mod_weight, residual_cot, normed_cot):
    latents, tokens, features = residual.shape
    rows = latents * tokens
    shard = proj_weight.shape[0]
    pieces = (blk // 2 - 1) * HALVES
    own_cond = lax.dynamic_slice_in_dim(
        condition, lax.axis_index("blk") * shard, shard, 1
    ).astype(F32)
    lat_rows = latents * COLUMN_BLOCKS // blk
    mod_cols = 3 * features // COLUMN_BLOCKS
    flat = lambda a: a.reshape(rows, features)
    big = jax.ShapeDtypeStruct((rows, features), BF16)
    anywhere = pl.BlockSpec(memory_space=pl.ANY)
    vmem = pl.BlockSpec(memory_space=pltpu.VMEM)
    small = pltpu.VMEM((blk, lat_rows, mod_cols), F32)
    wide = pltpu.VMEM((rows, features), BF16)
    dma = pltpu.SemaphoreType.DMA
    outs = pl.pallas_call(
        functools.partial(kernel, groups, blk, latents, tokens),
        out_shape=(big, big, big, jax.ShapeDtypeStruct((latents, shard), F32)),
        in_specs=[anywhere, anywhere, vmem, anywhere, anywhere, anywhere, anywhere],
        out_specs=(anywhere, anywhere, anywhere, vmem),
        scratch_shapes=[
            pltpu.VMEM((shard * blk, features), BF16),
            wide, wide, wide, wide,
            pltpu.VMEM((shard, 3 * features), BF16),
            pltpu.VMEM((rows, features), F32),
            pltpu.VMEM((latents, 1, 3 * features), F32),
            pltpu.VMEM((latents, 8, 3 * features), F32),
            small, small, small, small, small, small,
            dma((6,)), dma((10,)),
            dma((3, pieces)), dma((3, pieces)), dma((3, pieces)), dma((3, pieces)),
            dma((2,)),
            dma((2, blk)), dma((2, blk)), dma((2, blk)), dma((2, blk)),
        ],
        compiler_params=pltpu.CompilerParams(
            collective_id=0, has_side_effects=True, vmem_limit_bytes=60 * 2**20
        ),
        cost_estimate=pl.CostEstimate(
            flops=4 * rows * features * features, bytes_accessed=30 * 2**20, transcendentals=0
        ),
    )(
        flat(residual), flat(attention), own_cond, proj_weight, mod_weight,
        flat(residual_cot), flat(normed_cot),
    )
    return tuple(a.reshape(latents, tokens, features) for a in outs[:3]) + (outs[3],)


def solution(mesh):
    in_specs = (
        P("groups", "blk", None),
        P("groups", "blk", None),
        P("groups", None),
        P("blk", None),
        P("blk", None),
        P("groups", "blk", None),
        P("groups", "blk", None),
    )
    out_specs = (
        P("groups", "blk", None),
        P("groups", "blk", None),
        P("groups", "blk", None),
        P("groups", "blk"),
    )
    body = functools.partial(local, mesh.shape["groups"], mesh.shape["blk"])
    return jax.shard_map(body, mesh=mesh, in_specs=in_specs, out_specs=out_specs, check_vma=False)
```

time: 332 us -> 121 us (0.36)
  waiting for transfers between devices: 256 us -> 0 us
  Pallas kernels: 0 us -> 110 us
  matrix products: 38.5 us -> 0 us
  other arithmetic: 19.8 us -> 1.36 us
  between operations: 13.9 us -> 0.66 us
  local copies, waits for them, and re-layouts: 3.05 us -> 9.2 us
    psum x2 -> x0, waiting for transfers between devices: 156 us -> none  [the longest x1 90.5 us: local(): lax.psum(jnp.dot(own_act, mod_weight, preferred_element_type=jnp.float32)...]
    pallas_call x0 -> x1, Pallas kernels: none -> 110 us  [local(): pl.pallas_call(functools.partial(kernel, groups, blk, latents, tokens), o...]
    all_gather x1 -> x0, waiting for transfers between devices: 100 us -> none  [local(): lax.all_gather(proj_weight, 'blk', axis=0, tiled=True)]
    dot_general x4 -> x0, matrix products: 38.5 us -> none  [the longest x1 17.1 us: local(): jnp.dot(flat_attn, lax.all_gather(proj_weight, 'blk', axis=0, tiled=True)...]
    reduce_sum x3 -> x0, other arithmetic: 10.1 us -> none  [the longest x1 6.22 us: local(): jnp.sum(summed_grad * projected, axis=1)]
    unnamed x14 -> x10, local copies, waits for them, and re-layouts: 3.05 us -> 9.2 us
    convert_element_type x1, other arithmetic: 7.5 us -> 1.36 us  [local(): own_cond = lax.dynamic_slice_in_dim(condition, lax.axis_index('blk') * sh...]
  transfers between devices with their start and end apart: 3 -> 0, of which waited for: 3 -> 0; matrix products, arithmetic and copies ran while one was open for 7% -> 0% of each run, Pallas kernels for 0% -> 0%
where the time goes in v1:
time: 121 us
  Pallas kernels  110 us (91%)
  local copies, waits for them, and re-layouts  9.2 us (8%)
  other arithmetic  1.36 us (1%)
    pallas_call x1, Pallas kernels, local(): pl.pallas_call(functools.partial(kernel, groups, blk, latents, tokens), o...  110 us
    unnamed x10, local copies, waits for them, and re-layouts  9.2 us

profile of v1, /device:TPU:0, one launch (start us, length us, event | category | flops | bytes accessed | tf_op | source)
XLA Modules:
  0.0 120.8 jit_solution(5846040788537686764)
XLA Ops:
  0.6 1.4 %dynamic-slice_convert_fusion.cond = f32[4,192]{1,0:T(4,128)} fusion(bf16[4,3072]{1,0:T(4,128)(2,1)} %param.9, s32[]{:T(128)S(6)} %select_n.3), kind=kLoop, calls=%fused_computation | loop fusion | flops 768 | bytes 4612 | tf_op jit(solution)/shard_map/convert_element_type | solution.py:425
  2.0 109.6 %shard_map.102 = (bf16[512,3072]{1,0:T(8,128)(2,1)}, bf16[512,3072]{1,0:T(8,128)(2,1)}, bf16[512,3072]{1,0:T(8,128)(2,1)}, f32[4,192]{1,0:T(4,128)}) custom-call(bf16[512,3072]{1,0:T(8,128)(2,1)} %bitcast.10, bf16[512,3072]{1,0:T(8,128)(2,1)} %bitcast.11, f32[4,192]{1,0:T(4,128)} %dynamic-slice_convert_fusion.cond, bf16[192,3072]{1,0:T(8,128)(2,1)} %w_hbm.1, ...), custom_call_target="tpu_custom_call" | custom-call | flops 19327352832 | bytes 31457280 | tf_op jit(solution)/shard_map/pallas_call | solution.py:435
  111.6 0.0 copy-start.1
  111.6 3.9 %copy.15 = bf16[4,128,3072]{2,1,0:T(8,128)(2,1)} copy(bf16[4,128,3072]{2,1,0:T(8,128)(2,1)} %bitcast.9) | data formatting | bytes 6291456
  115.5 0.0 copy-done.1
  115.5 0.0 copy-start
  115.5 1.7 %copy.16 = bf16[4,128,3072]{2,1,0:T(8,128)(2,1)} copy(bf16[4,128,3072]{2,1,0:T(8,128)(2,1)S(1)} %bitcast.8) | data formatting | bytes 6291456
  117.2 1.4 %copy-done = bf16[512,3072]{1,0:T(8,128)(2,1)S(1)} copy-done((bf16[512,3072]{1,0:T(8,128)(2,1)S(1)}, bf16[512,3072]{1,0:T(8,128)(2,1)}, u32[]{:S(2)}) %copy-start) | copy-done | bytes 3145752
  118.6 0.0 copy-start.2
  118.6 1.7 %copy.17 = bf16[4,128,3072]{2,1,0:T(8,128)(2,1)} copy(bf16[4,128,3072]{2,1,0:T(8,128)(2,1)S(1)} %bitcast.7) | data formatting | bytes 6291456
  120.2 0.0 copy-done.2
  120.2 0.6 copy.18
Async XLA Ops:
  111.6 3.9 %copy-start.1 = (bf16[512,3072]{1,0:T(8,128)(2,1)S(1)}, bf16[512,3072]{1,0:T(8,128)(2,1)}, u32[]{:S(2)}) copy-start(bf16[512,3072]{1,0:T(8,128)(2,1)} %get-tuple-element.9) | copy-start | bytes 9437188
  115.5 3.0 %copy-start = (bf16[512,3072]{1,0:T(8,128)(2,1)S(1)}, bf16[512,3072]{1,0:T(8,128)(2,1)}, u32[]{:S(2)}) copy-start(bf16[512,3072]{1,0:T(8,128)(2,1)} %get-tuple-element.10) | copy-start | bytes 9437188
  118.6 1.7 %copy-start.2 = (f32[4,192]{1,0:T(4,128)S(1)}, f32[4,192]{1,0:T(4,128)}, u32[]{:S(2)}) copy-start(f32[4,192]{1,0:T(4,128)} %get-tuple-element.19) | copy-start | bytes 9220

commit v2 on v1

--- a/solution.py
+++ b/solution.py
@@ -14,15 +14,16 @@
 HALVES = 2
 COLUMN_BLOCKS = 8
 TILE = 32
+STORES = 4
 
 
 def kernel(
     groups, blk, latents, tokens,
     res_hbm, att_hbm, cond, w_hbm, modw_hbm, rcot_hbm, ncot_hbm,
-    nout_hbm, rgrad_hbm, agrad_hbm, cgrad,
-    w, att, res, rcot, ncot, modw, acc, mod, mgrad,
+    res, rcot, ncot, grads,
+    w, att, modw, acc, mod, mgrad,
     stage_a, land_a, full_a, stage_b, land_b, full_b,
-    load_sem, store_sem, ring_send, ring_recv, sib_send, sib_recv, own_sem,
+    load_sem, ring_send, ring_recv, sib_send, sib_recv, own_sem,
     rs_send, rs_recv, ag_send, ag_recv,
 ):
     rows, features = att.shape
@@ -349,28 +350,16 @@
 
     lax.fori_loop(0, rows // TILE, norm, 0)
 
-    stores = [
-        pltpu.make_async_copy(res, nout_hbm, store_sem.at[0]),
-        pltpu.make_async_copy(rcot, rgrad_hbm, store_sem.at[1]),
-    ]
-    for store in stores:
-        store.start()
-
     sum_begin(1, jnp.sum(mgrad[...], axis=1), stage_b, land_b)
 
     tiles = 8
     width = features // tiles
-
-    def back_store(n):
-        c = pl.ds(pl.multiple_of(n * width, width), width)
-        return pltpu.make_async_copy(ncot.at[:, c], agrad_hbm.at[:, c], store_sem.at[2 + n])
 
     def back(n, carry):
         k = pl.ds(pl.multiple_of(n * width, width), width)
         ncot[:, k] = lax.dot_general(
             att[...], w[k, :], (((1,), (1,)), ((), ())), preferred_element_type=F32
         ).astype(BF16)
-        back_store(n).start()
 
         @pl.when(n == 2)
         def _():
@@ -381,19 +370,9 @@
     lax.fori_loop(0, tiles, back, 0)
 
     def put_grad(lat, col, values):
-        mod[lat, :, pl.ds(col, mod_cols)] = values
+        grads[lat, :, pl.ds(col, mod_cols)] = values
 
     sum_end(1, stage_b, land_b, full_b, put_grad)
-    grads = jnp.concatenate([mod[i] for i in range(latents)], axis=0)
-    upper = grads.astype(BF16).astype(F32)
-    both = jnp.concatenate([upper, grads - upper], axis=0).astype(BF16)
-    product = lax.dot_general(
-        both, modw[...], (((1,), (1,)), ((), ())), preferred_element_type=F32
-    )
-    back_sum = product[:latents] + product[latents:]
-    gate = jax.nn.sigmoid(v)
-    slope = gate * (1.0 + v * (1.0 - gate))
-    cgrad[...] = slope * back_sum / math.sqrt(tokens * blk)
 
     def finish(i, carry):
         ring(i, 0).wait_send()
@@ -405,14 +384,34 @@
 
     lax.fori_loop(0, total, finish, 0)
     own_to_sibling(core).wait_send()
+
+def finish_kernel(
+    latents, seq_len, res, rcot, ncot, grads, cond, modw,
+    nout_hbm, rgrad_hbm, agrad_hbm, cgrad, store_sem,
+):
+    rows = res.shape[0]
+    part = rows // STORES
+    stores = []
+    for a, (src, dst) in enumerate(((res, nout_hbm), (rcot, rgrad_hbm), (ncot, agrad_hbm))):
+        for i in range(STORES):
+            r = pl.ds(i * part, part)
+            stores.append(
+                pltpu.make_async_copy(src.at[r], dst.at[r], store_sem.at[a * STORES + i])
+            )
+    for store in stores:
+        store.start()
+    total = jnp.concatenate([grads[i] for i in range(latents)], axis=0)
+    upper = total.astype(BF16).astype(F32)
+    both = jnp.concatenate([upper, total - upper], axis=0).astype(BF16)
+    product = lax.dot_general(
+        both, modw[...], (((1,), (1,)), ((), ())), preferred_element_type=F32
+    )
+    v = cond[...]
+    gate = jax.nn.sigmoid(v)
+    slope = gate * (1.0 + v * (1.0 - gate))
+    cgrad[...] = slope * (product[:latents] + product[latents:]) / math.sqrt(seq_len)
     for store in stores:
         store.wait()
-
-    def drain(n, carry):
-        back_store(n).wait()
-        return carry
-
-    lax.fori_loop(0, tiles, drain, 0)
 
 
 def local(groups, blk, residual, attention, condition, proj_weight, mod_weight, residual_cot, normed_cot):
@@ -427,31 +426,32 @@
     mod_cols = 3 * features // COLUMN_BLOCKS
     flat = lambda a: a.reshape(rows, features)
     big = jax.ShapeDtypeStruct((rows, features), BF16)
+    held = pltpu.VMEM((rows, features), BF16)
     anywhere = pl.BlockSpec(memory_space=pl.ANY)
     vmem = pl.BlockSpec(memory_space=pltpu.VMEM)
     small = pltpu.VMEM((blk, lat_rows, mod_cols), F32)
     wide = pltpu.VMEM((rows, features), BF16)
     dma = pltpu.SemaphoreType.DMA
-    outs = pl.pallas_call(
+    held_outs = pl.pallas_call(
         functools.partial(kernel, groups, blk, latents, tokens),
-        out_shape=(big, big, big, jax.ShapeDtypeStruct((latents, shard), F32)),
+        out_shape=(held, held, held, pltpu.VMEM((latents, 1, 3 * features), F32)),
         in_specs=[anywhere, anywhere, vmem, anywhere, anywhere, anywhere, anywhere],
-        out_specs=(anywhere, anywhere, anywhere, vmem),
+        out_specs=(vmem, vmem, vmem, vmem),
         scratch_shapes=[
             pltpu.VMEM((shard * blk, features), BF16),
-            wide, wide, wide, wide,
+            wide,
             pltpu.VMEM((shard, 3 * features), BF16),
             pltpu.VMEM((rows, features), F32),
             pltpu.VMEM((latents, 1, 3 * features), F32),
             pltpu.VMEM((latents, 8, 3 * features), F32),
             small, small, small, small, small, small,
-            dma((6,)), dma((10,)),
+            dma((6,)),
             dma((3, pieces)), dma((3, pieces)), dma((3, pieces)), dma((3, pieces)),
             dma((2,)),
             dma((2, blk)), dma((2, blk)), dma((2, blk)), dma((2, blk)),
         ],
         compiler_params=pltpu.CompilerParams(
-            collective_id=0, has_side_effects=True, vmem_limit_bytes=60 * 2**20
+            collective_id=0, has_side_effects=True, vmem_limit_bytes=48 * 2**20
         ),
         cost_estimate=pl.CostEstimate(
             flops=4 * rows * features * features, bytes_accessed=30 * 2**20, transcendentals=0
@@ -460,6 +460,14 @@
         flat(residual), flat(attention), own_cond, proj_weight, mod_weight,
         flat(residual_cot), flat(normed_cot),
     )
+    outs = pl.pallas_call(
+        functools.partial(finish_kernel, latents, tokens * blk),
+        out_shape=(big, big, big, jax.ShapeDtypeStruct((latents, shard), F32)),
+        in_specs=[vmem] * 6,
+        out_specs=(anywhere, anywhere, anywhere, vmem),
+        scratch_shapes=[dma((3 * STORES,))],
+        compiler_params=pltpu.CompilerParams(vmem_limit_bytes=16 * 2**20),
+    )(*held_outs, own_cond, mod_weight)
     return tuple(a.reshape(latents, tokens, features) for a in outs[:3]) + (outs[3],)
 
 

time: 121 us -> 115 us (0.950)
  local copies, waits for them, and re-layouts: 9.2 us -> 0.01 us
  Pallas kernels: 110 us -> 113 us
    unnamed x10 -> x4, local copies, waits for them, and re-layouts: 9.2 us -> 0.01 us
    pallas_call x0 -> x1, Pallas kernels: none -> 4.67 us  [local(): pl.pallas_call(functools.partial(finish_kernel, latents, tokens * blk), o...]
    pallas_call x1, Pallas kernels: 110 us -> 108 us  [local(): pl.pallas_call(functools.partial(kernel, groups, blk, latents, tokens), o...]
where the time goes in v2:
time: 115 us
  Pallas kernels  113 us (98%)
  other arithmetic  1.36 us (1%)
    pallas_call x1, Pallas kernels, local(): pl.pallas_call(functools.partial(kernel, groups, blk, latents, tokens), o...  108 us
    pallas_call x1, Pallas kernels, local(): pl.pallas_call(functools.partial(finish_kernel, latents, tokens * blk), o...  4.67 us

profile of v2, /device:TPU:0, one launch (start us, length us, event | category | flops | bytes accessed | tf_op | source)
XLA Modules:
  0.0 114.7 jit_solution(1354764816521124698)
XLA Ops:
  0.6 1.4 %dynamic-slice_convert_fusion.cond = f32[4,192]{1,0:T(4,128)} fusion(bf16[4,3072]{1,0:T(4,128)(2,1)} %param.9, s32[]{:T(128)S(6)} %select_n.3), kind=kLoop, calls=%fused_computation | loop fusion | flops 768 | bytes 4612 | tf_op jit(solution)/shard_map/convert_element_type | solution.py:424
  2.0 0.0 copy-start
  2.0 0.0 copy-start.1
  2.0 108.0 %shard_map.102 = (bf16[512,3072]{1,0:T(8,128)(2,1)S(1)}, bf16[512,3072]{1,0:T(8,128)(2,1)S(1)}, bf16[512,3072]{1,0:T(8,128)(2,1)S(1)}, f32[4,1,9216]{2,1,0:T(1,128)S(1)}) custom-call(bf16[512,3072]{1,0:T(8,128)(2,1)} %bitcast.7, bf16[512,3072]{1,0:T(8,128)(2,1)} %bitcast.8, f32[4,192]{1,0:T(4,128)} %dynamic-slice_convert_fusion.cond, ...), custom_call_target="tpu_custom_call" | custom-call | flops 19327352832 | bytes 31457280 | tf_op jit(solution)/shard_map/pallas_call | solution.py:435
  110.0 0.0 copy-done
  110.0 0.0 copy-done.1
  110.0 4.7 %shard_map.103 = (bf16[512,3072]{1,0:T(8,128)(2,1)}, bf16[512,3072]{1,0:T(8,128)(2,1)}, bf16[512,3072]{1,0:T(8,128)(2,1)}, f32[4,192]{1,0:T(4,128)}) custom-call(bf16[512,3072]{1,0:T(8,128)(2,1)S(1)} %get-tuple-element.12.res, bf16[512,3072]{1,0:T(8,128)(2,1)S(1)} %get-tuple-element.13.rcot, bf16[512,3072]{1,0:T(8,128)(2,1)S(1)} %get-tuple-element.14.ncot, ...), custom_call_target="tpu_custom_call" | custom-call | tf_op jit(solution)/shard_map/pallas_call | solution.py:463
Async XLA Ops:
  2.0 108.0 %copy-start = (bf16[192,9216]{1,0:T(8,128)(2,1)S(1)}, bf16[192,9216]{1,0:T(8,128)(2,1)}, u32[]{:S(2)}) copy-start(bf16[192,9216]{1,0:T(8,128)(2,1)} %modw.1) | copy-start | bytes 10616836
  2.0 108.0 %copy-start.1 = (f32[4,192]{1,0:T(4,128)S(1)}, f32[4,192]{1,0:T(4,128)}, u32[]{:S(2)}) copy-start(f32[4,192]{1,0:T(4,128)} %dynamic-slice_convert_fusion.cond) | copy-start | bytes 9220

commit v3 on v2

--- a/solution.py
+++ b/solution.py
@@ -20,7 +20,7 @@
 def kernel(
     groups, blk, latents, tokens,
     res_hbm, att_hbm, cond, w_hbm, modw_hbm, rcot_hbm, ncot_hbm,
-    res, rcot, ncot, grads,
+    res, rcot, ncot, grads, own,
     w, att, modw, acc, mod, mgrad,
     stage_a, land_a, full_a, stage_b, land_b, full_b,
     load_sem, ring_send, ring_recv, sib_send, sib_recv, own_sem,
@@ -30,6 +30,7 @@
     shard = w_hbm.shape[0]
     chip_rows = 2 * shard
     chips = blk // 2
+    overlapped = chip_rows % 128 == 0
     third = features // 3
     piece = shard // HALVES
     steps = chips - 1
@@ -202,13 +203,17 @@
         each_peer(lambda peer: spread(which, full, peer, me).wait_send())
 
     loads[1].wait()
-    v = cond[...]
+    if overlapped:
+        near = cond[:, pl.ds(pl.multiple_of(chip * chip_rows, chip_rows), chip_rows)].astype(F32)
+        v = jnp.where(core == 0, near[:, :shard], near[:, shard:])
+    else:
+        v = cond[...]
+    own[...] = v
     act = (v * jax.nn.sigmoid(v)).astype(BF16)
     sum_begin(0, jnp.dot(act, modw[...], preferred_element_type=F32), stage_a, land_a)
 
     acc[...] = jnp.zeros_like(acc)
     loads[2].wait()
-    overlapped = chip_rows % 128 == 0
 
     def multiply(step, way):
         if not overlapped:
@@ -270,23 +275,23 @@
 
             multiply(step, 2)
 
-        @pl.when(i == 1)
+        @pl.when(i == 2 * HALVES)
         def _():
             sum_middle(0, stage_a, land_a, full_a)
 
-        @pl.when(i == 5)
+        @pl.when(i == 4 * HALVES)
         def _():
             sum_end(0, stage_a, land_a, full_a, put_mod)
 
         return carry
 
     lax.fori_loop(0, total, turn, 0)
-    cross_in(total - 1).wait_recv()
-    to_sibling(total - 1, 2, core).start()
     from_sibling(steps, 0)
     multiply(steps, 0)
     from_sibling(steps, 1)
     multiply(steps, 1)
+    cross_in(total - 1).wait_recv()
+    to_sibling(total - 1, 2, core).start()
     from_sibling(steps, 2)
     multiply(steps, 2)
 
@@ -419,9 +424,10 @@
     rows = latents * tokens
     shard = proj_weight.shape[0]
     pieces = (blk // 2 - 1) * HALVES
-    own_cond = lax.dynamic_slice_in_dim(
-        condition, lax.axis_index("blk") * shard, shard, 1
-    ).astype(F32)
+    if 2 * shard % 128:
+        condition = lax.dynamic_slice_in_dim(
+            condition, lax.axis_index("blk") * shard, shard, 1
+        ).astype(F32)
     lat_rows = latents * COLUMN_BLOCKS // blk
     mod_cols = 3 * features // COLUMN_BLOCKS
     flat = lambda a: a.reshape(rows, features)
@@ -434,9 +440,10 @@
     dma = pltpu.SemaphoreType.DMA
     held_outs = pl.pallas_call(
         functools.partial(kernel, groups, blk, latents, tokens),
-        out_shape=(held, held, held, pltpu.VMEM((latents, 1, 3 * features), F32)),
+        out_shape=(held, held, held, pltpu.VMEM((latents, 1, 3 * features), F32),
+            pltpu.VMEM((latents, shard), F32)),
         in_specs=[anywhere, anywhere, vmem, anywhere, anywhere, anywhere, anywhere],
-        out_specs=(vmem, vmem, vmem, vmem),
+        out_specs=(vmem,) * 5,
         scratch_shapes=[
             pltpu.VMEM((shard * blk, features), BF16),
             wide,
@@ -457,7 +464,7 @@
             flops=4 * rows * features * features, bytes_accessed=30 * 2**20, transcendentals=0
         ),
     )(
-        flat(residual), flat(attention), own_cond, proj_weight, mod_weight,
+        flat(residual), flat(attention), condition, proj_weight, mod_weight,
         flat(residual_cot), flat(normed_cot),
     )
     outs = pl.pallas_call(
@@ -467,7 +474,7 @@
         out_specs=(anywhere, anywhere, anywhere, vmem),
         scratch_shapes=[dma((3 * STORES,))],
         compiler_params=pltpu.CompilerParams(vmem_limit_bytes=16 * 2**20),
-    )(*held_outs, own_cond, mod_weight)
+    )(*held_outs, mod_weight)
     return tuple(a.reshape(latents, tokens, features) for a in outs[:3]) + (outs[3],)
 
 

time: 115 us -> 113 us (0.983)
  other arithmetic: 1.36 us -> 0 us
    convert_element_type x1 -> x0, other arithmetic: 1.36 us -> none  [local(): own_cond = lax.dynamic_slice_in_dim(condition, lax.axis_index('blk') * sh...]
where the time goes in v3:
time: 113 us; the launch traced here: 112 us
  Pallas kernels  112 us (99%)
    pallas_call x1, Pallas kernels, local(): pl.pallas_call(functools.partial(kernel, groups, blk, latents, tokens), o...  107 us
    pallas_call x1, Pallas kernels, local(): pl.pallas_call(functools.partial(finish_kernel, latents, tokens * blk), o...  4.67 us

profile of v3, /device:TPU:0, one launch (start us, length us, event | category | flops | bytes accessed | tf_op | source)
XLA Modules:
  0.0 112.3 jit_solution(17054217088898939145)
XLA Ops:
  0.6 0.0 copy-start
  0.6 107.0 %shard_map.102 = (bf16[512,3072]{1,0:T(8,128)(2,1)S(1)}, bf16[512,3072]{1,0:T(8,128)(2,1)S(1)}, bf16[512,3072]{1,0:T(8,128)(2,1)S(1)}, f32[4,1,9216]{2,1,0:T(1,128)S(1)}, f32[4,192]{1,0:T(4,128)S(1)}) custom-call(bf16[512,3072]{1,0:T(8,128)(2,1)} %bitcast.7, bf16[512,3072]{1,0:T(8,128)(2,1)} %bitcast.8, bf16[4,3072]{1,0:T(4,128)(2,1)} %cond.1, ...), custom_call_target="tpu_custom_call" | custom-call | flops 19327352832 | bytes 31457280 | tf_op jit(solution)/shard_map/pallas_call | solution.py:441
  107.7 0.0 copy-done
  107.7 4.7 %shard_map.103 = (bf16[512,3072]{1,0:T(8,128)(2,1)}, bf16[512,3072]{1,0:T(8,128)(2,1)}, bf16[512,3072]{1,0:T(8,128)(2,1)}, f32[4,192]{1,0:T(4,128)}) custom-call(bf16[512,3072]{1,0:T(8,128)(2,1)S(1)} %get-tuple-element.13.res, bf16[512,3072]{1,0:T(8,128)(2,1)S(1)} %get-tuple-element.14.rcot, bf16[512,3072]{1,0:T(8,128)(2,1)S(1)} %get-tuple-element.15.ncot, ...), custom_call_target="tpu_custom_call" | custom-call | tf_op jit(solution)/shard_map/pallas_call | solution.py:470
Async XLA Ops:
  0.6 107.0 %copy-start = (bf16[192,9216]{1,0:T(8,128)(2,1)S(1)}, bf16[192,9216]{1,0:T(8,128)(2,1)}, u32[]{:S(2)}) copy-start(bf16[192,9216]{1,0:T(8,128)(2,1)} %modw.1) | copy-start | bytes 10616836
